TPU v7x, 32 devices: a whole 2x2x4 slice. The times are simulated.
32 devices in a mesh: parts: 2 (over x), row: 4 (over y, core), col: 4 (over z).
Axes of the slice: x: 2, y: 2, z: 4, core: 2. Of those that a mesh axis runs over, the one named last changes fastest.
Arguments:
- object_field: float32 [2, 2048, 2048], P(None, ('parts', 'row'), 'col'), parts along dimension 1, may hold values from -4 to 4
- probe_field: float32 [2, 128, 128], replicated, may hold values from -4 to 4
- amplitudes: float32 [4, 4, 24, 128, 128], P('row', 'col', 'parts'), parts along dimension 2, may hold values from 0.1 to 3
- positions: int32 [4, 4, 4, 12], P('row', 'col', 'parts'), parts along dimension 2, may hold values from 0 to 2047, as said below
- counts: int32 [8, 4], P(('parts', 'row'), 'col'), parts along dimension 0, may hold values from 1 to 12, 32 in all within a row
Outputs:
- object_out: float32 [2, 2048, 2048], P(None, ('parts', 'row'), 'col'), parts along dimension 1
- probe_out: float32 [4, 128, 128], P('parts'), parts along dimension 0
There are 2 independent parts, one for each index of `parts`. A program takes and returns all parts, laid end to end along the dimension named above; an argument that names none is the same for every part. Nothing has to cross between parts.
Inputs may be any that keep to these rules, and one draw needn't show every extreme that they name: positions[a, b, 0, s] lies in a * 256 to (a + 1) * 256 - 1 and positions[a, b, 1, s] in b * 512 to (b + 1) * 512 - 1: every slot's centre lies in its own tile; centres sit on a grid of pitch 64 plus a jitter of 0 to 63 pixels along each dimension; slot 0 of tile (0, 0) is centred at (0, 0) and the last slot of the last tile at (1023, 2047). Slots 0 to counts[a, b] - 1 of tile (a, b) are recorded, the rest are to be ignored; each row of tiles holds 64 recorded patterns.
All inputs are finite; a program needn't handle non-finite values. No bound on the sum of `counts` on one device may be relied on, other than what follows from the above.
Results may differ from a plain program's by a relative error of at most 0.0003.
Values sent between devices are 32-bit elements; how exact they have to be, the bound alone decides.
A program may use at most 64 MiB of HBM per device.

v0:
```python
import math

import jax
import jax.numpy as jnp
from jax import lax
from jax.experimental import pallas as pl
from jax.experimental.pallas import tpu as pltpu
from jax.sharding import PartitionSpec as P

ITERS = 2


step_object = 0.25
step_probe = 0.5
floor_amp = 0.5
LANES = 128


def padded(cells, sides, width):
    for axis, dim in sides:
        count = lax.axis_size(axis)
        ends = count - 1
        head = lax.slice_in_dim(cells, 0, width, axis=dim)
        tail = lax.slice_in_dim(cells, cells.shape[dim] - width, cells.shape[dim], axis=dim)
        cells = jnp.concatenate(
            [
                lax.ppermute(tail, axis, [(i, (i + 1) % count) for i in range(ends)]),
                cells,
                lax.ppermute(head, axis, [((i + 1) % count, i) for i in range(ends)]),
            ],
            axis=dim,
        )
    return cells


def from_behind(value, axis, steps):
    count = lax.axis_size(axis)
    initial, last = (max(0, -steps), min(count, count - steps))
    return lax.ppermute(value, axis, [(source, source + steps) for source in range(initial, last)])


def tables(size):
    index = jnp.arange(size, dtype=jnp.int32)
    wrapped = index[:, None] * index[None, :] % size
    angle = 2.0 * math.pi / size * wrapped.astype(jnp.float32)
    scaling = 1.0 / math.sqrt(size)
    cosine, sine = (jnp.cos(angle) * scaling, jnp.sin(angle) * scaling)
    both = jnp.stack(
        [
            jnp.block([[cosine, -sine], [sine, cosine]]),
            jnp.block([[cosine, sine], [-sine, cosine]]),
        ]
    )
    high = lax.reduce_precision(both, 8, 7)
    return (high.astype(jnp.bfloat16), (both - high).astype(jnp.bfloat16))


def extend_object(object_field, rim_width):
    return padded(object_field, (("row", 1), ("col", 2)), rim_width)


def fold_edges(grid, tile_rows, tile_cols, rim_width):
    from_left = from_behind(grid[:, :, tile_cols + rim_width :], "col", 1)
    from_right = from_behind(grid[:, :, :rim_width], "col", -1)
    middle = grid[:, :, rim_width : tile_cols + rim_width]
    middle = middle.at[:, :, :rim_width].add(from_left)
    middle = middle.at[:, :, tile_cols - rim_width :].add(from_right)
    from_above = from_behind(middle[:, tile_rows + rim_width :, :], "row", 1)
    from_below = from_behind(middle[:, :rim_width, :], "row", -1)
    inner = middle[:, rim_width : tile_rows + rim_width, :]
    inner = inner.at[:, :rim_width, :].add(from_above)
    inner = inner.at[:, tile_rows - rim_width :, :].add(from_below)
    return inner


def update_probe(probe_field, grad_probe, scaling):
    total = lax.psum(grad_probe, ("row", "col"))
    return probe_field - scaling * total


def split(value):
    high = value.astype(jnp.bfloat16)
    return high, (value - high.astype(jnp.float32)).astype(jnp.bfloat16)


def dot(a, b):
    return jnp.dot(a, b, preferred_element_type=jnp.float32)


def times_right(value, table_high, table_low):
    high, low = split(value)
    return dot(high, table_high) + dot(low, table_high) + dot(high, table_low)


def times_left(table_high, table_low, value):
    high, low = split(value)
    return dot(table_high, high) + dot(table_low, high) + dot(table_high, low)


def swap_blocks(value):
    n = LANES
    return jnp.concatenate(
        [
            jnp.concatenate([value[:n, :n], value[n:, :n]], axis=1),
            jnp.concatenate([value[:n, n:], value[n:, n:]], axis=1),
        ],
        axis=0,
    )


def take_patch(source, part, place):
    n = LANES
    high_row, low_row, base, shift = place
    rows = n + 8
    lane = lax.broadcasted_iota(jnp.int32, (rows, n), 1)
    left = source[part, pl.ds(high_row, rows), pl.ds(base, n)]
    right = source[part, pl.ds(high_row, rows), pl.ds(base + n, n)]
    both = pltpu.roll(jnp.where(lane >= shift, left, right), (n - shift) % n, 1)
    turned = pltpu.roll(both.reshape(rows // 8, 8, n), (8 - low_row) % 8, 1)
    line = lax.broadcasted_iota(jnp.int32, (n // 8, 8, n), 1)
    return jnp.where(line < 8 - low_row, turned[:-1], turned[1:]).reshape(n, n)


def add_piece(grid, part, place, piece):
    n = LANES
    high_row, low_row, base, shift = place
    rows = n + 8
    turned = pltpu.roll(pltpu.roll(piece, shift, 1).reshape(n // 8, 8, n), low_row, 1)
    none = jnp.zeros((1, 8, n), jnp.float32)
    line = lax.broadcasted_iota(jnp.int32, (rows // 8, 8, n), 1)
    tall = jnp.where(
        line >= low_row,
        jnp.concatenate([turned, none], axis=0),
        jnp.concatenate([none, turned], axis=0),
    ).reshape(rows, n)
    lane = lax.broadcasted_iota(jnp.int32, (rows, n), 1)
    at_rows = pl.ds(high_row, rows)
    grid[part, at_rows, pl.ds(base, n)] += jnp.where(lane >= shift, tall, 0.0)
    grid[part, at_rows, pl.ds(base + n, n)] += jnp.where(lane >= shift, 0.0, tall)


def slots_kernel(
    rows, cols, count, extended, probe, amplitude, high_tables, low_tables, grid, grad_probe
):
    n = LANES
    slot_count = amplitude.shape[0]
    grid[...] = jnp.zeros_like(grid)
    probe_real = probe[0]
    probe_imag = probe[1]
    probe_sum_real = jnp.zeros((n, n), jnp.float32)
    probe_sum_imag = jnp.zeros((n, n), jnp.float32)
    a_high, b_high = high_tables[0], high_tables[1]
    a_low, b_low = low_tables[0], low_tables[1]
    for pair in range(slot_count // 2):
        patches = []
        exits = []
        places = []
        for slot in (2 * pair, 2 * pair + 1):
            row_at = rows[slot]
            col_at = cols[slot]
            place = (
                pl.multiple_of(row_at // 8 * 8, 8),
                row_at % 8,
                pl.multiple_of(col_at // n * n, n),
                col_at % n,
            )
            patch = [take_patch(extended, part, place) for part in range(2)]
            patches.append(patch)
            places.append(place)
            exits.append(
                jnp.concatenate(
                    [
                        probe_real * patch[0] - probe_imag * patch[1],
                        probe_real * patch[1] + probe_imag * patch[0],
                    ],
                    axis=1,
                )
            )
        wave = times_right(jnp.concatenate(exits, axis=0), a_high, a_low)
        far = times_left(b_high, b_low, swap_blocks(wave))
        far_real, far_imag = far[:n], far[n:]
        measured = jnp.concatenate([amplitude[2 * pair], amplitude[2 * pair + 1]], axis=1)
        power = far_real * far_real + far_imag * far_imag
        keeping = 1.0 - measured * lax.rsqrt(jnp.maximum(power, floor_amp * floor_amp))
        kept = jnp.concatenate([far_real * keeping, far_imag * keeping], axis=0)
        back = times_left(a_high, a_low, kept)
        change = times_right(swap_blocks(back), b_high, b_low)
        for k in range(2):
            usable = jnp.where(2 * pair + k < count[0], 1.0, 0.0)
            change_real = change[k * n : (k + 1) * n, :n] * usable
            change_imag = change[k * n : (k + 1) * n, n:] * usable
            object_real, object_imag = patches[k]
            probe_sum_real += object_real * change_real + object_imag * change_imag
            probe_sum_imag += object_real * change_imag - object_imag * change_real
            pieces = (
                probe_real * change_real + probe_imag * change_imag,
                probe_real * change_imag - probe_imag * change_real,
            )
            for part in range(2):
                add_piece(grid, part, places[k], pieces[part])
    grad_probe[0] = probe_sum_real
    grad_probe[1] = probe_sum_imag


def gradients(rows, cols, count, extended, probe, amplitude, high_tables, low_tables):
    smem = pl.BlockSpec(memory_space=pltpu.SMEM)
    vmem = pl.BlockSpec(memory_space=pltpu.VMEM)
    return pl.pallas_call(
        slots_kernel,
        out_shape=(
            jax.ShapeDtypeStruct(extended.shape, jnp.float32),
            jax.ShapeDtypeStruct(probe.shape, jnp.float32),
        ),
        in_specs=[smem] * 3 + [vmem] * 5,
        out_specs=(vmem, vmem),
        compiler_params=pltpu.CompilerParams(vmem_limit_bytes=40 * 1024 * 1024),
    )(rows, cols, count, extended, probe, amplitude, high_tables, low_tables)


def shards(object_field, probe_field, amplitudes, positions, counts):
    tile_rows = object_field.shape[1]
    tile_cols = object_field.shape[2]
    patch_size = probe_field.shape[-1]
    rim_width = patch_size // 2
    slot_count = amplitudes.shape[2]
    recorded = lax.axis_size("row") * lax.axis_size("col") * (2 * slot_count // 3)
    scaling = step_probe / recorded
    high_tables, low_tables = tables(patch_size)
    start_rows = positions[0, 0, 0] - lax.axis_index("row") * tile_rows
    start_cols = positions[0, 0, 1] - lax.axis_index("col") * tile_cols
    measured = amplitudes[0, 0]
    for iteration in range(ITERS):
        extended = extend_object(object_field, rim_width)
        grid, grad_probe = gradients(
            start_rows, start_cols, counts[0], extended, probe_field, measured,
            high_tables, low_tables,
        )
        grad_object = fold_edges(grid, tile_rows, tile_cols, rim_width)
        object_field = object_field - step_object * grad_object
        probe_field = update_probe(probe_field, grad_probe, scaling)
    return (object_field, probe_field)


def solution(mesh):
    return jax.shard_map(
        shards,
        mesh=mesh,
        in_specs=(
            P(None, ("parts", "row"), "col"),
            P(),
            P("row", "col", "parts", None, None),
            P("row", "col", "parts", None),
            P(("parts", "row"), "col"),
        ),
        out_specs=(P(None, ("parts", "row"), "col"), P("parts", None, None)),
        check_vma=False,
    )
```

profile of v0, /device:TPU:0, one launch (start us, length us, event | category | flops | bytes accessed | tf_op | source)
XLA Modules:
  0.0 277.8 jit_solution(4167333898161537150)
XLA Ops:
  8.4 1.3 collective-permute-start.1
  9.7 3.0 %collective-permute-start = (f32[2,64,512]{2,1,0:T(8,128)S(1)}, f32[2,64,512]{2,1,0:T(8,128)S(1)}, u32[]{:S(2)}, u32[]{:S(2)}) collective-permute-start(f32[2,64,512]{2,1,0:T(8,128)S(1)} %get-tuple-element.121), channel_id=1, source_target_pairs={{0,4},{4,8},{8,12},{1,5},{5,9},{9,13},{2,6},{6,10},{10,14},{3,7},{... | collective-permute-start | bytes 786440 | tf_op jit(solution)/shard_map/ppermute | solution.py:27
  14.4 5.0 %collective-permute-start.2 = (f32[2,384,64]{2,1,0:T(8,128)S(1)}, f32[2,384,64]{2,1,0:T(8,128)S(1)}, u32[]{:S(2)}, u32[]{:S(2)}) collective-permute-start(f32[2,384,64]{2,1,0:T(8,128)S(1)} %get-tuple-element.116), channel_id=1, source_target_pairs={{0,1},{1,2},{2,3},{4,5},{5,6},{6,7},{8,9},{9,10},{10,11},{12,13},{... | collective-permute-start | bytes 589832 | tf_op jit(solution)/shard_map/ppermute | solution.py:27
  20.7 5.9 %collective-permute-done.2 = f32[2,384,64]{2,1,0:T(8,128)S(1)} collective-permute-done((f32[2,384,64]{2,1,0:T(8,128)S(1)}, f32[2,384,64]{2,1,0:T(8,128)S(1)}, u32[]{:S(2)}, u32[]{:S(2)}) %collective-permute-start.2) | collective-permute-done | bytes 196640 | tf_op jit(solution)/shard_map/ppermute | solution.py:27
  26.7 4.7 %collective-permute-done.3 = f32[2,384,64]{2,1,0:T(8,128)S(1)} collective-permute-done((f32[2,384,64]{2,1,0:T(8,128)S(1)}, f32[2,384,64]{2,1,0:T(8,128)S(1)}, u32[]{:S(2)}, u32[]{:S(2)}) %collective-permute-start.3) | collective-permute-done | bytes 196640 | tf_op jit(solution)/shard_map/ppermute | solution.py:29
  32.1 7.4 %shard_map.68 = (f32[2,384,640]{2,1,0:T(8,128)S(1)}, f32[2,128,128]{2,1,0:T(8,128)}) custom-call(s32[12]{0:T(128)S(1)} %get-tuple-element.127.rows, s32[12]{0:T(128)S(1)} %get-tuple-element.126.cols, s32[1]{0:T(128)} %bitcast.10.count, f32[2,384,640]{2,1,0:T(8,128)S(1)} %pad_maximum_fusion.extended, f32[2,128,128]{2,1,0:T(8,128)S(1)} %copy-done.1, ...), custom_call_target="tpu_custom_call" | custom-call | tf_op jit(solution)/shard_map/pallas_call | solution.py:208
  40.3 3.5 %collective-permute-start.4 = (f32[2,384,64]{2,1,0:T(8,128)S(1)}, f32[2,384,64]{2,1,0:T(8,128)S(1)}, u32[]{:S(2)}, u32[]{:S(2)}) collective-permute-start(f32[2,384,64]{2,1,0:T(8,128)S(1)} %get-tuple-element.109), channel_id=1, source_target_pairs={{0,1},{1,2},{2,3},{4,5},{5,6},{6,7},{8,9},{9,10},{10,11},{12,13},{... | collective-permute-start | bytes 589832 | tf_op jit(solution)/shard_map/ppermute | solution.py:39
  45.6 7.0 %collective-permute-done.4 = f32[2,384,64]{2,1,0:T(8,128)S(1)} collective-permute-done((f32[2,384,64]{2,1,0:T(8,128)S(1)}, f32[2,384,64]{2,1,0:T(8,128)S(1)}, u32[]{:S(2)}, u32[]{:S(2)}) %collective-permute-start.4) | collective-permute-done | bytes 196640 | tf_op jit(solution)/shard_map/ppermute | solution.py:39
  52.8 1.6 scatter-add.26
  54.3 3.8 %collective-permute-done.5 = f32[2,384,64]{2,1,0:T(8,128)} collective-permute-done((f32[2,384,64]{2,1,0:T(8,128)}, f32[2,384,64]{2,1,0:T(8,128)}, u32[]{:S(2)}, u32[]{:S(2)}) %collective-permute-start.5) | collective-permute-done | bytes 196640 | tf_op jit(solution)/shard_map/ppermute | solution.py:39
  59.3 1.6 scatter-add.29
  60.9 2.1 collective-permute-start.6
  63.0 1.4 collective-permute-start.7
  64.6 2.0 collective-permute-done.7
  67.7 6.2 %collective-permute-start.8 = (f32[2,64,512]{2,1,0:T(8,128)}, f32[2,64,512]{2,1,0:T(8,128)S(1)}, u32[]{:S(2)}, u32[]{:S(2)}) collective-permute-start(f32[2,64,512]{2,1,0:T(8,128)} %get-tuple-element.118), channel_id=1, source_target_pairs={{0,4},{4,8},{8,12},{1,5},{5,9},{9,13},{2,6},{6,10},{10,14},{3,7},{... | collective-permute-start | bytes 786440 | tf_op jit(solution)/shard_map/ppermute | solution.py:27
  75.3 2.0 collective-permute-done.9
  78.3 3.5 %collective-permute-start.10 = (f32[2,384,64]{2,1,0:T(8,128)}, f32[2,384,64]{2,1,0:T(8,128)S(1)}, u32[]{:S(2)}, u32[]{:S(2)}) collective-permute-start(f32[2,384,64]{2,1,0:T(8,128)} %get-tuple-element.112), channel_id=1, source_target_pairs={{0,1},{1,2},{2,3},{4,5},{5,6},{6,7},{8,9},{9,10},{10,11},{12,13},{... | collective-permute-start | bytes 589832 | tf_op jit(solution)/shard_map/ppermute | solution.py:27
  81.8 1.5 collective-permute-start.11
  83.3 79.2 %all-reduce.3.cloned.1.call-done = f32[2,128,128]{2,1,0:T(8,128)} async-done(((f32[2,128,128]{2,1,0:T(8,128)}), f32[2,128,128]{2,1,0:T(8,128)}) %all-reduce.3.cloned.1.call-update) | async-done | bytes 131088 | tf_op jit(solution)/shard_map/psum | solution.py:77
  163.5 1.7 pad_maximum_fusion.1.extended
  165.1 7.4 %shard_map.69 = (f32[2,384,640]{2,1,0:T(8,128)S(1)}, f32[2,128,128]{2,1,0:T(8,128)}) custom-call(s32[12]{0:T(128)S(1)} %get-tuple-element.127.rows, s32[12]{0:T(128)S(1)} %get-tuple-element.126.cols, s32[1]{0:T(128)} %bitcast.11.count, f32[2,384,640]{2,1,0:T(8,128)S(1)} %pad_maximum_fusion.1.extended, f32[2,128,128]{2,1,0:T(8,128)S(1)} %multiply_subtract_fusion.3.probe, ...), custom_call_target="tpu_custom_call" | custom-call | tf_op jit(solution)/shard_map/pallas_call | solution.py:208
  172.7 6.0 %collective-permute-start.12 = (f32[2,384,64]{2,1,0:T(8,128)S(1)}, f32[2,384,64]{2,1,0:T(8,128)S(1)}, u32[]{:S(2)}, u32[]{:S(2)}) collective-permute-start(f32[2,384,64]{2,1,0:T(8,128)S(1)} %get-tuple-element.107), channel_id=1, source_target_pairs={{0,1},{1,2},{2,3},{4,5},{5,6},{6,7},{8,9},{9,10},{10,11},{12,13},{... | collective-permute-start | bytes 589832 | tf_op jit(solution)/shard_map/ppermute | solution.py:39
  178.7 1.7 slice.282
  181.7 2.3 collective-permute-done.12
  184.1 2.0 scatter-add.34
  186.1 4.7 %collective-permute-done.13 = f32[2,384,64]{2,1,0:T(8,128)} collective-permute-done((f32[2,384,64]{2,1,0:T(8,128)S(1)}, f32[2,384,64]{2,1,0:T(8,128)}, u32[]{:S(2)}, u32[]{:S(2)}) %collective-permute-start.13) | collective-permute-done | bytes 196640 | tf_op jit(solution)/shard_map/ppermute | solution.py:39
  192.1 2.2 scatter-add.35
  195.4 1.3 collective-permute-start.14
  196.7 1.3 collective-permute-start.15
  198.0 67.7 %all-reduce.5.cloned.1.call-done = f32[2,128,128]{2,1,0:T(8,128)} async-done(((f32[2,128,128]{2,1,0:T(8,128)}), f32[2,128,128]{2,1,0:T(8,128)}) %all-reduce.5.cloned.1.call-update) | async-done | bytes 131088 | tf_op jit(solution)/shard_map/psum | solution.py:77
  265.7 1.6 multiply_subtract_fusion.2
  267.2 1.4 slice.303
  (60 shorter events, 18.9 us)
Async XLA Ops:
  7.2 6.9 %copy-start.4 = (f32[2,256,512]{2,1,0:T(8,128)S(1)}, f32[2,256,512]{2,1,0:T(8,128)}, u32[]{:S(2)}) copy-start(f32[2,256,512]{2,1,0:T(8,128)} %param.21) | copy-start | bytes 3145732
  7.2 155.3 %all-reduce.3.cloned.1.call-start = ((), (), s32[]{:S(2)}) async-start(), calls=%async_computation | async-start | bytes 262144 | tf_op jit(solution)/shard_map/psum | solution.py:77
  8.4 5.8 %collective-permute-start.1 = (f32[2,64,512]{2,1,0:T(8,128)S(1)}, f32[2,64,512]{2,1,0:T(8,128)S(1)}, u32[]{:S(2)}, u32[]{:S(2)}) collective-permute-start(f32[2,64,512]{2,1,0:T(8,128)S(1)} %get-tuple-element.120), channel_id=1, source_target_pairs={{4,0},{8,4},{12,8},{5,1},{9,5},{13,9},{6,2},{10,6},{14,10},{7,3},{... | collective-permute-start | bytes 786440 | tf_op jit(solution)/shard_map/ppermute | solution.py:29
  9.7 4.4 %collective-permute-start = (f32[2,64,512]{2,1,0:T(8,128)S(1)}, f32[2,64,512]{2,1,0:T(8,128)S(1)}, u32[]{:S(2)}, u32[]{:S(2)}) collective-permute-start(f32[2,64,512]{2,1,0:T(8,128)S(1)} %get-tuple-element.121), channel_id=1, source_target_pairs={{0,4},{4,8},{8,12},{1,5},{5,9},{9,13},{2,6},{6,10},{10,14},{3,7},{... | collective-permute-start | bytes 786440 | tf_op jit(solution)/shard_map/ppermute | solution.py:27
  14.2 6.5 %copy-start.6 = (s32[1,1,2,12]{3,2,1,0:T(2,128)S(1)}, s32[1,1,2,12]{3,2,1,0:T(2,128)}, u32[]{:S(2)}) copy-start(s32[1,1,2,12]{3,2,1,0:T(2,128)} %param.24) | copy-start | bytes 292
  14.4 12.3 %collective-permute-start.2 = (f32[2,384,64]{2,1,0:T(8,128)S(1)}, f32[2,384,64]{2,1,0:T(8,128)S(1)}, u32[]{:S(2)}, u32[]{:S(2)}) collective-permute-start(f32[2,384,64]{2,1,0:T(8,128)S(1)} %get-tuple-element.116), channel_id=1, source_target_pairs={{0,1},{1,2},{2,3},{4,5},{5,6},{6,7},{8,9},{9,10},{10,11},{12,13},{... | collective-permute-start | bytes 589832 | tf_op jit(solution)/shard_map/ppermute | solution.py:27
  19.4 12.0 %collective-permute-start.3 = (f32[2,384,64]{2,1,0:T(8,128)S(1)}, f32[2,384,64]{2,1,0:T(8,128)S(1)}, u32[]{:S(2)}, u32[]{:S(2)}) collective-permute-start(f32[2,384,64]{2,1,0:T(8,128)S(1)} %get-tuple-element.117), channel_id=1, source_target_pairs={{1,0},{2,1},{3,2},{5,4},{6,5},{7,6},{9,8},{10,9},{11,10},{13,12},{... | collective-permute-start | bytes 589832 | tf_op jit(solution)/shard_map/ppermute | solution.py:29
  20.7 11.4 %copy-start = (f32[1,1,12,128,128]{4,3,2,1,0:T(8,128)S(1)}, f32[1,1,12,128,128]{4,3,2,1,0:T(8,128)}, u32[]{:S(2)}) copy-start(f32[1,1,12,128,128]{4,3,2,1,0:T(8,128)} %param.23) | copy-start | bytes 2359300
  20.7 11.4 %copy-start.1 = (f32[2,128,128]{2,1,0:T(8,128)S(1)}, f32[2,128,128]{2,1,0:T(8,128)}, u32[]{:S(2)}) copy-start(f32[2,128,128]{2,1,0:T(8,128)} %probe.1) | copy-start | bytes 393220
  40.3 12.2 %collective-permute-start.4 = (f32[2,384,64]{2,1,0:T(8,128)S(1)}, f32[2,384,64]{2,1,0:T(8,128)S(1)}, u32[]{:S(2)}, u32[]{:S(2)}) collective-permute-start(f32[2,384,64]{2,1,0:T(8,128)S(1)} %get-tuple-element.109), channel_id=1, source_target_pairs={{0,1},{1,2},{2,3},{4,5},{5,6},{6,7},{8,9},{9,10},{10,11},{12,13},{... | collective-permute-start | bytes 589832 | tf_op jit(solution)/shard_map/ppermute | solution.py:39
  44.3 13.8 %collective-permute-start.5 = (f32[2,384,64]{2,1,0:T(8,128)}, f32[2,384,64]{2,1,0:T(8,128)}, u32[]{:S(2)}, u32[]{:S(2)}) collective-permute-start(f32[2,384,64]{2,1,0:T(8,128)} %get-tuple-element.108), channel_id=1, source_target_pairs={{1,0},{2,1},{3,2},{5,4},{6,5},{7,6},{9,8},{10,9},{11,10},{13,12},{... | collective-permute-start | bytes 589832 | tf_op jit(solution)/shard_map/ppermute | solution.py:39
  60.9 3.7 %collective-permute-start.6 = (f32[2,64,512]{2,1,0:T(8,128)S(1)}, f32[2,64,512]{2,1,0:T(8,128)S(1)}, u32[]{:S(2)}, u32[]{:S(2)}) collective-permute-start(f32[2,64,512]{2,1,0:T(8,128)S(1)} %get-tuple-element.115), channel_id=1, source_target_pairs={{0,4},{4,8},{8,12},{1,5},{5,9},{9,13},{2,6},{6,10},{10,14},{3,7},{... | collective-permute-start | bytes 786440 | tf_op jit(solution)/shard_map/ppermute | solution.py:39
  63.0 3.6 %copy-start.5 = (f32[2,256,512]{2,1,0:T(8,128)S(1)}, f32[2,256,512]{2,1,0:T(8,128)}, u32[]{:S(2)}) copy-start(f32[2,256,512]{2,1,0:T(8,128)} %param.21) | copy-start | bytes 3145732
  63.0 3.6 %collective-permute-start.7 = (f32[2,64,512]{2,1,0:T(8,128)S(1)}, f32[2,64,512]{2,1,0:T(8,128)S(1)}, u32[]{:S(2)}, u32[]{:S(2)}) collective-permute-start(f32[2,64,512]{2,1,0:T(8,128)S(1)} %get-tuple-element.114), channel_id=1, source_target_pairs={{4,0},{8,4},{12,8},{5,1},{9,5},{13,9},{6,2},{10,6},{14,10},{7,3},{... | collective-permute-start | bytes 786440 | tf_op jit(solution)/shard_map/ppermute | solution.py:39
  66.9 96.5 %copy-start.2 = (f32[2,256,512]{2,1,0:T(8,128)}, f32[2,256,512]{2,1,0:T(8,128)S(1)}, u32[]{:S(2)}) copy-start(f32[2,256,512]{2,1,0:T(8,128)S(1)} %multiply_subtract_fusion.1) | copy-start | bytes 3145732
  67.7 7.6 %collective-permute-start.8 = (f32[2,64,512]{2,1,0:T(8,128)}, f32[2,64,512]{2,1,0:T(8,128)S(1)}, u32[]{:S(2)}, u32[]{:S(2)}) collective-permute-start(f32[2,64,512]{2,1,0:T(8,128)} %get-tuple-element.118), channel_id=1, source_target_pairs={{0,4},{4,8},{8,12},{1,5},{5,9},{9,13},{2,6},{6,10},{10,14},{3,7},{... | collective-permute-start | bytes 786440 | tf_op jit(solution)/shard_map/ppermute | solution.py:27
  73.9 3.4 %collective-permute-start.9 = (f32[2,64,512]{2,1,0:T(8,128)S(1)}, f32[2,64,512]{2,1,0:T(8,128)S(1)}, u32[]{:S(2)}, u32[]{:S(2)}) collective-permute-start(f32[2,64,512]{2,1,0:T(8,128)S(1)} %get-tuple-element.119), channel_id=1, source_target_pairs={{4,0},{8,4},{12,8},{5,1},{9,5},{13,9},{6,2},{10,6},{14,10},{7,3},{... | collective-permute-start | bytes 786440 | tf_op jit(solution)/shard_map/ppermute | solution.py:29
  75.2 190.4 %all-reduce.5.cloned.1.call-start = ((), (), s32[]{:S(2)}) async-start(), calls=%async_computation.1 | async-start | bytes 262144 | tf_op jit(solution)/shard_map/psum | solution.py:77
  78.3 85.1 %collective-permute-start.10 = (f32[2,384,64]{2,1,0:T(8,128)}, f32[2,384,64]{2,1,0:T(8,128)S(1)}, u32[]{:S(2)}, u32[]{:S(2)}) collective-permute-start(f32[2,384,64]{2,1,0:T(8,128)} %get-tuple-element.112), channel_id=1, source_target_pairs={{0,1},{1,2},{2,3},{4,5},{5,6},{6,7},{8,9},{9,10},{10,11},{12,13},{... | collective-permute-start | bytes 589832 | tf_op jit(solution)/shard_map/ppermute | solution.py:27
  81.8 81.6 %collective-permute-start.11 = (f32[2,384,64]{2,1,0:T(8,128)}, f32[2,384,64]{2,1,0:T(8,128)}, u32[]{:S(2)}, u32[]{:S(2)}) collective-permute-start(f32[2,384,64]{2,1,0:T(8,128)} %get-tuple-element.113), channel_id=1, source_target_pairs={{1,0},{2,1},{3,2},{5,4},{6,5},{7,6},{9,8},{10,9},{11,10},{13,12},{... | collective-permute-start | bytes 589832 | tf_op jit(solution)/shard_map/ppermute | solution.py:29
  172.7 11.3 %collective-permute-start.12 = (f32[2,384,64]{2,1,0:T(8,128)S(1)}, f32[2,384,64]{2,1,0:T(8,128)S(1)}, u32[]{:S(2)}, u32[]{:S(2)}) collective-permute-start(f32[2,384,64]{2,1,0:T(8,128)S(1)} %get-tuple-element.107), channel_id=1, source_target_pairs={{0,1},{1,2},{2,3},{4,5},{5,6},{6,7},{8,9},{9,10},{10,11},{12,13},{... | collective-permute-start | bytes 589832 | tf_op jit(solution)/shard_map/ppermute | solution.py:39
  180.4 10.5 %collective-permute-start.13 = (f32[2,384,64]{2,1,0:T(8,128)S(1)}, f32[2,384,64]{2,1,0:T(8,128)}, u32[]{:S(2)}, u32[]{:S(2)}) collective-permute-start(f32[2,384,64]{2,1,0:T(8,128)S(1)} %get-tuple-element.106), channel_id=1, source_target_pairs={{1,0},{2,1},{3,2},{5,4},{6,5},{7,6},{9,8},{10,9},{11,10},{13,12},{... | collective-permute-start | bytes 589832 | tf_op jit(solution)/shard_map/ppermute | solution.py:39
  195.4 73.3 %collective-permute-start.14 = (f32[2,64,512]{2,1,0:T(8,128)S(1)}, f32[2,64,512]{2,1,0:T(8,128)S(1)}, u32[]{:S(2)}, u32[]{:S(2)}) collective-permute-start(f32[2,64,512]{2,1,0:T(8,128)S(1)} %get-tuple-element.111), channel_id=1, source_target_pairs={{0,4},{4,8},{8,12},{1,5},{5,9},{9,13},{2,6},{6,10},{10,14},{3,7},{... | collective-permute-start | bytes 786440 | tf_op jit(solution)/shard_map/ppermute | solution.py:39
  196.7 72.9 %collective-permute-start.15 = (f32[2,64,512]{2,1,0:T(8,128)S(1)}, f32[2,64,512]{2,1,0:T(8,128)S(1)}, u32[]{:S(2)}, u32[]{:S(2)}) collective-permute-start(f32[2,64,512]{2,1,0:T(8,128)S(1)} %get-tuple-element.110), channel_id=1, source_target_pairs={{4,0},{8,4},{12,8},{5,1},{9,5},{13,9},{6,2},{10,6},{14,10},{7,3},{... | collective-permute-start | bytes 786440 | tf_op jit(solution)/shard_map/ppermute | solution.py:39
  267.2 2.5 copy-start.3
Sparse Core Ops, SparseCore 0:
  75.3 87.1 all-reduce.2
  180.5 85.1 all-reduce.4
where the time goes:
time: 280 us; the launch traced here: 278 us
  waiting for transfers between devices  179 us (64%)
  starting transfers between devices  41.3 us (15%)
  local copies, waits for them, and re-layouts  15.3 us (5%)
  between operations  15.1 us (5%)
  Pallas kernels  14.8 us (5%)
  other arithmetic  11.9 us (4%)
    psum x2, waiting for transfers between devices, update_probe(): total = lax.psum(grad_probe, ('row', 'col'))  147 us
    ppermute x8, waiting for transfers between devices, from_behind(): lax.ppermute(value, axis, [(source, source + steps) for source in range(i...  19.7 us
    ppermute x8, starting transfers between devices, from_behind(): lax.ppermute(value, axis, [(source, source + steps) for source in range(i...  18.2 us
    ppermute x4, starting transfers between devices, padded(): lax.ppermute(tail, axis, [(i, (i + 1) % count) for i in range(ends)])  17.6 us
    pallas_call x2, Pallas kernels, gradients(): pl.pallas_call(slots_kernel, out_shape=(jax.ShapeDtypeStruct(extended.sha...  14.8 us
    ppermute x4, waiting for transfers between devices, padded(): lax.ppermute(head, axis, [((i + 1) % count, i) for i in range(ends)])  6.75 us
    ppermute x4, waiting for transfers between devices, padded(): lax.ppermute(tail, axis, [(i, (i + 1) % count) for i in range(ends)])  5.95 us
  transfers between devices with their start and end apart: 18, of which 10 were waited for; matrix products, arithmetic and copies ran while one was open for 6% of the time, Pallas kernels for 0%

commit v1 on v0

--- a/solution.py
+++ b/solution.py
@@ -1,3 +1,4 @@
+import functools
 import math
 
 import jax
@@ -14,29 +15,6 @@
 step_probe = 0.5
 floor_amp = 0.5
 LANES = 128
-
-
-def padded(cells, sides, width):
-    for axis, dim in sides:
-        count = lax.axis_size(axis)
-        ends = count - 1
-        head = lax.slice_in_dim(cells, 0, width, axis=dim)
-        tail = lax.slice_in_dim(cells, cells.shape[dim] - width, cells.shape[dim], axis=dim)
-        cells = jnp.concatenate(
-            [
-                lax.ppermute(tail, axis, [(i, (i + 1) % count) for i in range(ends)]),
-                cells,
-                lax.ppermute(head, axis, [((i + 1) % count, i) for i in range(ends)]),
-            ],
-            axis=dim,
-        )
-    return cells
-
-
-def from_behind(value, axis, steps):
-    count = lax.axis_size(axis)
-    initial, last = (max(0, -steps), min(count, count - steps))
-    return lax.ppermute(value, axis, [(source, source + steps) for source in range(initial, last)])
 
 
 def tables(size):
@@ -53,29 +31,6 @@
     )
     high = lax.reduce_precision(both, 8, 7)
     return (high.astype(jnp.bfloat16), (both - high).astype(jnp.bfloat16))
-
-
-def extend_object(object_field, rim_width):
-    return padded(object_field, (("row", 1), ("col", 2)), rim_width)
-
-
-def fold_edges(grid, tile_rows, tile_cols, rim_width):
-    from_left = from_behind(grid[:, :, tile_cols + rim_width :], "col", 1)
-    from_right = from_behind(grid[:, :, :rim_width], "col", -1)
-    middle = grid[:, :, rim_width : tile_cols + rim_width]
-    middle = middle.at[:, :, :rim_width].add(from_left)
-    middle = middle.at[:, :, tile_cols - rim_width :].add(from_right)
-    from_above = from_behind(middle[:, tile_rows + rim_width :, :], "row", 1)
-    from_below = from_behind(middle[:, :rim_width, :], "row", -1)
-    inner = middle[:, rim_width : tile_rows + rim_width, :]
-    inner = inner.at[:, :rim_width, :].add(from_above)
-    inner = inner.at[:, tile_rows - rim_width :, :].add(from_below)
-    return inner
-
-
-def update_probe(probe_field, grad_probe, scaling):
-    total = lax.psum(grad_probe, ("row", "col"))
-    return probe_field - scaling * total
 
 
 def split(value):
@@ -217,27 +172,459 @@
     )(rows, cols, count, extended, probe, amplitude, high_tables, low_tables)
 
 
+MESH = pl.DeviceIdType.MESH
+
+
+class Links:
+    def __init__(self, sizes, send_sem, recv_sem):
+        self.sizes = sizes
+        self.send_sem = send_sem
+        self.recv_sem = recv_sem
+        self.at = {axis: lax.axis_index(axis) for axis in sizes}
+        self.used = 0
+
+    def has(self, axis, step):
+        return self.at[axis] > 0 if step < 0 else self.at[axis] < self.sizes[axis] - 1
+
+    def peer(self, axis, step):
+        size = self.sizes[axis]
+        return lax.rem(self.at[axis] + (step + size), size)
+
+    def greet(self, everyone):
+        barrier = pltpu.get_barrier_semaphore()
+        if everyone:
+            for axis, size in self.sizes.items():
+                for step in range(1, size):
+                    pl.semaphore_signal(
+                        barrier, inc=1, device_id={axis: self.peer(axis, step)}, device_id_type=MESH
+                    )
+            pl.semaphore_wait(barrier, sum(size - 1 for size in self.sizes.values()))
+            return
+        for axis in self.sizes:
+            for step in (-1, 1):
+                @pl.when(self.has(axis, step))
+                def signal():
+                    pl.semaphore_signal(
+                        barrier, inc=1, device_id={axis: self.peer(axis, step)}, device_id_type=MESH
+                    )
+        peers = 0
+        for axis in self.sizes:
+            for step in (-1, 1):
+                peers = peers + jnp.where(self.has(axis, step), 1, 0)
+        pl.semaphore_wait(barrier, peers)
+
+    def copy(self, src, dst, axis, step):
+        number = self.used
+        self.used += 1
+        return pltpu.make_async_remote_copy(
+            src_ref=src,
+            dst_ref=dst,
+            send_sem=self.send_sem.at[number],
+            recv_sem=self.recv_sem.at[number],
+            device_id={axis: self.peer(axis, step)},
+            device_id_type=MESH,
+        )
+
+    def edge(self, src, dst, axis, step):
+        return Edge(self, self.copy(src, dst, axis, step), axis, step)
+
+
+class Edge:
+    def __init__(self, links, copy, axis, step):
+        self.links, self.copy, self.axis, self.step = links, copy, axis, step
+
+    def start(self):
+        pl.when(self.links.has(self.axis, self.step))(lambda: self.copy.start())
+
+    def wait_send(self):
+        pl.when(self.links.has(self.axis, self.step))(lambda: self.copy.wait_send())
+
+    def wait_recv(self):
+        pl.when(self.links.has(self.axis, -self.step))(lambda: self.copy.wait_recv())
+
+
+def clear(links, axis, step, ref):
+    @pl.when(jnp.logical_not(links.has(axis, step)))
+    def fill():
+        ref[...] = jnp.zeros(ref.shape, ref.dtype)
+
+
+STEPS = (-1, 1)
+
+
+def halo_kernel(sizes, tile, ext, band_out, band_in, corner_out, corner_in, send_sem, recv_sem):
+    n = LANES
+    half = n // 2
+    tile_rows, tile_cols = tile.shape[1:]
+    last = tile_cols + n
+    links = Links(sizes, send_sem, recv_sem)
+    links.greet(False)
+    rows = []
+    for step in STEPS:
+        src = tile.at[:, pl.ds(0 if step < 0 else tile_rows - half, half), :]
+        to = tile_rows + half if step < 0 else 0
+        rows.append(
+            links.edge(src, ext.at[:, pl.ds(to, half), pl.ds(n, tile_cols)], "row", step)
+        )
+    lane = lax.broadcasted_iota(jnp.int32, (tile_rows, n), 1)
+    bands = []
+    for k, step in enumerate(STEPS):
+        at = 0 if step < 0 else tile_cols - n
+        real = tile[0, :, at : at + n]
+        imag = pltpu.roll(tile[1, :, at : at + n], half, 1)
+        low, high = (real, imag) if step < 0 else (imag, real)
+        band_out[k] = jnp.where(lane < half, low, high)
+        clear(links, "col", -step, band_in.at[k])
+        band = links.edge(band_out.at[k], band_in.at[k], "col", step)
+        band.start()
+        bands.append(band)
+    for row in rows:
+        row.start()
+    for k, step in enumerate(STEPS):
+        clear(links, "row", -step, corner_in.at[k])
+        to = tile_rows + half if step < 0 else 0
+        clear(links, "row", -step, ext.at[:, pl.ds(to, half), pl.ds(n, tile_cols)])
+    ext[:, half : half + tile_rows, n : n + tile_cols] = tile[...]
+    for k, step in enumerate(STEPS):
+        bands[k].wait_recv()
+        got = band_in[k]
+        back = pltpu.roll(got, half, 1)
+        at = last if step < 0 else 0
+        keep = lane < half if step < 0 else lane >= half
+        ext[0, half : half + tile_rows, at : at + n] = jnp.where(keep, got, 0.0)
+        ext[1, half : half + tile_rows, at : at + n] = jnp.where(keep, back, 0.0)
+    corners = []
+    narrow = lax.broadcasted_iota(jnp.int32, (half, n), 1)
+    for k, step in enumerate(STEPS):
+        at = half if step < 0 else tile_rows
+        for part in range(2):
+            corner_out[k, part] = jnp.where(
+                narrow >= half,
+                ext[part, at : at + half, :n],
+                ext[part, at : at + half, last : last + n],
+            )
+        corner = links.edge(corner_out.at[k], corner_in.at[k], "row", step)
+        corner.start()
+        corners.append(corner)
+    for k, step in enumerate(STEPS):
+        corners[k].wait_recv()
+        to = tile_rows + half if step < 0 else 0
+        for part in range(2):
+            got = corner_in[k, part]
+            ext[part, to : to + half, :n] = jnp.where(narrow >= half, got, 0.0)
+            ext[part, to : to + half, last : last + n] = jnp.where(narrow < half, got, 0.0)
+        rows[k].wait_recv()
+    for edge in bands + rows + corners:
+        edge.wait_send()
+
+
+class ProbeSum:
+    def __init__(self, links, scaling, probe, gradient, new_probe, shares, sums, total):
+        self.links, self.scaling = links, scaling
+        self.probe, self.new_probe = probe, new_probe
+        self.shares, self.sums, self.total = shares, sums, total
+        self.count = gradient.shape[0] // links.sizes["row"]
+        self.mine = self.share(links.at["row"])
+        self.gradient = gradient
+        self.copies = []
+        self.first = []
+        for step in range(1, links.sizes["row"]):
+            src = gradient.at[self.share(links.peer("row", step)), :]
+            self.first.append(links.copy(src, shares.at[step - 1], "row", step))
+        for copy in self.first:
+            copy.start()
+
+    def share(self, owner):
+        return pl.ds(pl.multiple_of(owner * self.count, self.count), self.count)
+
+    def across(self):
+        links = self.links
+        value = self.gradient[self.mine, :]
+        for k, copy in enumerate(self.first):
+            copy.wait_recv()
+            value = value + self.shares[k]
+        own = links.at["col"]
+        self.sums[own] = value
+        self.second = []
+        for step in range(1, links.sizes["col"]):
+            self.second.append(links.copy(self.sums.at[own], self.sums.at[own], "col", step))
+        for copy in self.second:
+            copy.start()
+
+    def spread(self):
+        links = self.links
+        for copy in self.second:
+            copy.wait_recv()
+        value = self.sums[0]
+        for k in range(1, links.sizes["col"]):
+            value = value + self.sums[k]
+        self.new_probe[self.mine, :] = self.probe[self.mine, :] - self.scaling * value
+        self.third = []
+        for step in range(1, links.sizes["row"]):
+            ref = self.new_probe.at[self.mine, :]
+            self.third.append(links.copy(ref, ref, "row", step))
+        for copy in self.third:
+            copy.start()
+
+    def finish(self):
+        for copy in self.third:
+            copy.wait_recv()
+        for copy in self.first + self.second + self.third:
+            copy.wait_send()
+
+
+def middle_kernel(
+    sizes, scaling, ext, grid, probe, gradient, new_ext, new_probe,
+    edge_out, edge_in, inner_out, inner_in, side_out, side_in,
+    shares, sums, total, send_sem, recv_sem,
+):
+    n = LANES
+    half = n // 2
+    high = ext.shape[1]
+    last = ext.shape[2] - n
+    links = Links(sizes, send_sem, recv_sem)
+    links.greet(True)
+    summed = ProbeSum(links, scaling, probe, gradient, new_probe, shares, sums, total)
+    upper = lax.broadcasted_iota(jnp.int32, (n, n), 1) >= half
+
+    def block(part, at, k):
+        return grid[part, at : at + n, k : k + n]
+
+    def band(part, at, side):
+        base = 0 if side == 0 else last - n
+        return jnp.where(upper, block(part, at, base), block(part, at, base + n))
+
+    tops = (0, high - n)
+    edges = []
+    for k, step in enumerate(STEPS):
+        for part in range(2):
+            for side in range(2):
+                edge_out[k, part, side] = band(part, tops[k], side)
+        clear(links, "row", -step, edge_in.at[k])
+        edge = links.edge(edge_out.at[k], edge_in.at[k], "row", step)
+        edge.start()
+        edges.append(edge)
+    sides = []
+    for k, step in enumerate(STEPS):
+        for part in range(2):
+            side_out[k, 1, part] = band(part, n, k)
+        clear(links, "col", -step, side_in.at[k])
+        side = links.edge(side_out.at[k, 1], side_in.at[k, 1], "col", step)
+        side.start()
+        sides.append(side)
+    inners = []
+    for k, step in enumerate(STEPS):
+        for part in range(2):
+            inner_out[k, part, :, :n] = jnp.where(
+                upper, block(part, tops[k], n), block(part, tops[k], last - n)
+            )
+            inner_out[k, part, :, n:] = grid[part, tops[k] : tops[k] + n, 2 * n : last - n]
+        clear(links, "row", -step, inner_in.at[k])
+        inner = links.edge(inner_out.at[k], inner_in.at[k], "row", step)
+        inner.start()
+        inners.append(inner)
+    summed.across()
+    for k, step in enumerate(STEPS):
+        edges[1 - k].wait_recv()
+        for side, way in enumerate(STEPS):
+            for part in range(2):
+                side_out[side, 2 * k, part] = edge_out[k, part, side] + edge_in[1 - k, part, side]
+            corner = links.edge(side_out.at[side, 2 * k], side_in.at[side, 2 * k], "col", way)
+            corner.start()
+            sides.append(corner)
+    summed.spread()
+    for edge in inners + sides:
+        edge.wait_recv()
+    for k in range(3):
+        at = k * n
+        for part in range(2):
+            ends = [side_out[side, k, part] + side_in[1 - side, k, part] for side in range(2)]
+            if k == 1:
+                mixed = jnp.where(upper, block(part, at, n), block(part, at, last - n))
+                flat = grid[part, at : at + n, 2 * n : last - n]
+            else:
+                mixed = inner_out[k // 2, part, :, :n] + inner_in[1 - k // 2, part, :, :n]
+                flat = inner_out[k // 2, part, :, n:] + inner_in[1 - k // 2, part, :, n:]
+
+            def put(lo, hi, value):
+                new_ext[part, at : at + n, lo:hi] = (
+                    ext[part, at : at + n, lo:hi] - step_object * value
+                )
+
+            put(0, n, jnp.where(upper, ends[0], 0.0))
+            put(n, 2 * n, jnp.where(upper, mixed, ends[0]))
+            put(2 * n, last - n, flat)
+            put(last - n, last, jnp.where(upper, ends[1], mixed))
+            put(last, last + n, jnp.where(upper, 0.0, ends[1]))
+    clear(links, "row", -1, new_ext.at[:, pl.ds(0, half), :])
+    clear(links, "row", 1, new_ext.at[:, pl.ds(high - half, half), :])
+    clear(links, "col", -1, new_ext.at[:, :, pl.ds(0, n)])
+    clear(links, "col", 1, new_ext.at[:, :, pl.ds(last, n)])
+    for edge in edges + inners + sides:
+        edge.wait_send()
+    summed.finish()
+
+
+def final_kernel(
+    sizes, scaling, ext, grid, probe, gradient, tile, new_probe,
+    rim_out, rim_in, flat_in, mid_out, mid_in, end_out, end_in,
+    shares, sums, total, send_sem, recv_sem,
+):
+    n = LANES
+    half = n // 2
+    high = ext.shape[1]
+    last = ext.shape[2] - n
+    tile_rows, tile_cols = tile.shape[1:]
+    links = Links(sizes, send_sem, recv_sem)
+    links.greet(True)
+    summed = ProbeSum(links, scaling, probe, gradient, new_probe, shares, sums, total)
+    upper = lax.broadcasted_iota(jnp.int32, (half, n), 1) >= half
+    tall = lax.broadcasted_iota(jnp.int32, (n, n), 1) >= half
+    outer = (0, high - half)
+    inner = (half, high - n)
+    rims = []
+    flats = []
+    for k, step in enumerate(STEPS):
+        at = outer[k]
+        for part in range(2):
+            rim_out[k, part] = jnp.where(
+                upper, grid[part, at : at + half, :n], grid[part, at : at + half, last:]
+            )
+        clear(links, "row", -step, rim_in.at[k])
+        rim = links.edge(rim_out.at[k], rim_in.at[k], "row", step)
+        rim.start()
+        rims.append(rim)
+        clear(links, "row", -step, flat_in.at[k])
+        flats.append(
+            links.edge(
+                grid.at[:, pl.ds(at, half), pl.ds(n, tile_cols)], flat_in.at[k], "row", step
+            )
+        )
+
+    def fuse(mask, side, real, imag):
+        turned = pltpu.roll(imag, half, 1)
+        return jnp.where(mask, real, turned) if side == 0 else jnp.where(mask, turned, real)
+
+    middles = []
+    for side, way in enumerate(STEPS):
+        at = 0 if side == 0 else last
+        mid_out[side] = fuse(
+            tall, side, grid[0, n : high - n, at : at + n], grid[1, n : high - n, at : at + n]
+        )
+        clear(links, "col", -way, mid_in.at[side])
+        clear(links, "col", -way, end_in.at[side])
+        middle = links.edge(mid_out.at[side], mid_in.at[side], "col", way)
+        middle.start()
+        middles.append(middle)
+    for flat in flats:
+        flat.start()
+    summed.across()
+    for k in range(2):
+        rims[1 - k].wait_recv()
+        at = inner[k]
+        for side, way in enumerate(STEPS):
+            base = 0 if side == 0 else last
+            values = [
+                grid[part, at : at + half, base : base + n] + rim_in[1 - k, part]
+                for part in range(2)
+            ]
+            end_out[side, k] = fuse(upper, side, values[0], values[1])
+            end = links.edge(end_out.at[side, k], end_in.at[side, k], "col", way)
+            end.start()
+            middles.append(end)
+    tile[:, half : tile_rows - half, :] = (
+        ext[:, n : high - n, n:last] - step_object * grid[:, n : high - n, n:last]
+    )
+    summed.spread()
+    for k in range(2):
+        flats[1 - k].wait_recv()
+        at = inner[k]
+        tile[:, at - half : at, :] = ext[:, at : at + half, n:last] - step_object * (
+            grid[:, at : at + half, n:last] + flat_in[1 - k]
+        )
+    for middle in middles:
+        middle.wait_recv()
+
+    def land(at, count, side, value, mask):
+        base = tile_cols - n if side == 0 else 0
+        keep = mask if side == 0 else jnp.logical_not(mask)
+        turned = pltpu.roll(value, half, 1)
+        for part, piece in enumerate((value, turned)):
+            tile[part, at : at + count, base : base + n] -= step_object * jnp.where(
+                keep, piece, 0.0
+            )
+
+    for side in range(2):
+        land(half, n, side, mid_in[side], tall)
+        for k in range(2):
+            land(inner[k] - half, half, side, end_in[side, k], upper)
+    for edge in rims + flats + middles:
+        edge.wait_send()
+    summed.finish()
+
+
+def remote(kernel, collective_id, sizes, outs, scratch, copies, *operands):
+    vmem = pl.BlockSpec(memory_space=pltpu.VMEM)
+    return pl.pallas_call(
+        kernel,
+        out_shape=[jax.ShapeDtypeStruct(shape, jnp.float32) for shape in outs],
+        in_specs=[vmem] * len(operands),
+        out_specs=[vmem] * len(outs),
+        scratch_shapes=[pltpu.VMEM(shape, jnp.float32) for shape in scratch]
+        + [pltpu.SemaphoreType.DMA((copies,))] * 2,
+        compiler_params=pltpu.CompilerParams(
+            collective_id=collective_id,
+            has_side_effects=True,
+            vmem_limit_bytes=40 * 1024 * 1024,
+        ),
+    )(*operands)
+
+
 def shards(object_field, probe_field, amplitudes, positions, counts):
     tile_rows = object_field.shape[1]
     tile_cols = object_field.shape[2]
-    patch_size = probe_field.shape[-1]
-    rim_width = patch_size // 2
+    n = probe_field.shape[-1]
+    half = n // 2
     slot_count = amplitudes.shape[2]
-    recorded = lax.axis_size("row") * lax.axis_size("col") * (2 * slot_count // 3)
+    sizes = {axis: lax.axis_size(axis) for axis in ("row", "col")}
+    recorded = sizes["row"] * sizes["col"] * (2 * slot_count // 3)
     scaling = step_probe / recorded
-    high_tables, low_tables = tables(patch_size)
+    high_tables, low_tables = tables(n)
     start_rows = positions[0, 0, 0] - lax.axis_index("row") * tile_rows
-    start_cols = positions[0, 0, 1] - lax.axis_index("col") * tile_cols
+    start_cols = positions[0, 0, 1] - lax.axis_index("col") * tile_cols + half
     measured = amplitudes[0, 0]
+    wide = (2, tile_rows + n, tile_cols + 2 * n)
+    share = 2 * n // sizes["row"]
+    probe_scratch = [
+        (sizes["row"] - 1, share, n), (sizes["col"], share, n), (8, n),
+    ]
+    probe_copies = 2 * (sizes["row"] - 1) + sizes["col"] - 1
+    (extended,) = remote(
+        functools.partial(halo_kernel, sizes), 0, sizes, [wide],
+        [(2, tile_rows, n)] * 2 + [(2, 2, half, n)] * 2, 6, object_field,
+    )
     for iteration in range(ITERS):
-        extended = extend_object(object_field, rim_width)
         grid, grad_probe = gradients(
             start_rows, start_cols, counts[0], extended, probe_field, measured,
             high_tables, low_tables,
         )
-        grad_object = fold_edges(grid, tile_rows, tile_cols, rim_width)
-        object_field = object_field - step_object * grad_object
-        probe_field = update_probe(probe_field, grad_probe, scaling)
+        operands = (
+            extended, grid, probe_field.reshape(2 * n, n), grad_probe.reshape(2 * n, n)
+        )
+        if iteration < ITERS - 1:
+            extended, probe_field = remote(
+                functools.partial(middle_kernel, sizes, scaling), 1, sizes, [wide, (2 * n, n)],
+                [(2, 2, 2, n, n)] * 2 + [(2, 2, n, tile_cols - n)] * 2 + [(2, 3, 2, n, n)] * 2
+                + probe_scratch, 10 + probe_copies, *operands,
+            )
+        else:
+            object_field, probe_field = remote(
+                functools.partial(final_kernel, sizes, scaling), 2, sizes,
+                [object_field.shape, (2 * n, n)],
+                [(2, 2, half, n)] * 2 + [(2, 2, half, tile_cols)] + [(2, n, n)] * 2
+                + [(2, 2, half, n)] * 2 + probe_scratch, 10 + probe_copies, *operands,
+            )
+        probe_field = probe_field.reshape(2, n, n)
     return (object_field, probe_field)
 
 

time: 280 us -> 58.7 us (0.21)
  waiting for transfers between devices: 179 us -> 0 us
  starting transfers between devices: 41.3 us -> 0 us
  Pallas kernels: 14.8 us -> 54 us
  local copies, waits for them, and re-layouts: 15.3 us -> 1.64 us
  between operations: 15.1 us -> 1.48 us
  other arithmetic: 11.9 us -> 1.42 us
    psum x2 -> x0, waiting for transfers between devices: 147 us -> none  [update_probe(): total = lax.psum(grad_probe, ('row', 'col'))]
    ppermute x16 -> x0, starting transfers between devices: 41.2 us -> none  [the longest x8 18.2 us: from_behind(): lax.ppermute(value, axis, [(source, source + steps) for source in range(i...]
    pallas_call x0 -> x3, Pallas kernels: none -> 40.2 us  [remote(): pl.pallas_call(kernel, out_shape=[jax.ShapeDtypeStruct(shape, jnp.float32...]
    ppermute x16 -> x0, waiting for transfers between devices: 32.4 us -> none  [the longest x8 19.7 us: from_behind(): lax.ppermute(value, axis, [(source, source + steps) for source in range(i...]
    slice x11 -> x0, local copies, waits for them, and re-layouts: 7.85 us -> none  [the longest x2 2.13 us: fold_edges(): middle = grid[:, :, rim_width:tile_cols + rim_width]]
    scatter-add x4 -> x0, local copies, waits for them, and re-layouts: 7.34 us -> none  [the longest x2 3.74 us: fold_edges(): middle = middle.at[:, :, tile_cols - rim_width:].add(from_right)]
    sub x5 -> x0, other arithmetic: 3.93 us -> none  [the longest x2 2.5 us: update_probe(): return probe_field - scaling * total]
  transfers between devices with their start and end apart: 18 -> 0, of which waited for: 10 -> 0; matrix products, arithmetic and copies ran while one was open for 6% -> 0% of each run, Pallas kernels for 0% -> 0%
where the time goes in v1:
time: 58.7 us; the launch traced here: 58.5 us
  Pallas kernels  54 us (92%)
  local copies, waits for them, and re-layouts  1.64 us (3%)
  between operations  1.48 us (3%)
  other arithmetic  1.42 us (2%)
    pallas_call x3, Pallas kernels, remote(): pl.pallas_call(kernel, out_shape=[jax.ShapeDtypeStruct(shape, jnp.float32...  40.2 us
    pallas_call x2, Pallas kernels, gradients(): pl.pallas_call(slots_kernel, out_shape=(jax.ShapeDtypeStruct(extended.sha...  13.8 us
    unnamed x8, local copies, waits for them, and re-layouts  1.64 us

profile of v1, /device:TPU:0, one launch (start us, length us, event | category | flops | bytes accessed | tf_op | source)
XLA Modules:
  0.0 58.5 jit_solution(10715549102314520389)
XLA Ops:
  0.6 0.0 copy-start.1
  1.4 0.8 %add_bitcast_fusion = (s32[12]{0:T(128)S(1)}, s32[12]{0:T(128)S(1)}) fusion(s32[1,1,2,12]{3,2,1,0:T(2,128)} %param.8, s32[]{:T(128)S(6)} %mul.100, s32[]{:T(128)S(6)} %mul.99), kind=kLoop, calls=%fused_computation.24 | loop fusion | flops 36 | bytes 200 | tf_op jit(solution)/shard_map/add | solution.py:594
  2.1 0.3 fusion.11
  2.4 0.3 sine_multiply_fusion
  2.7 0.0 copy-start
  2.7 0.0 copy-start.2
  2.8 0.1 fusion
  2.8 0.0 copy-done.1
  2.8 9.7 %shard_map.68.extended.ext = f32[2,384,768]{2,1,0:T(8,128)S(1)} custom-call(f32[2,256,512]{2,1,0:T(8,128)S(1)} %copy-done.1), custom_call_target="tpu_custom_call" | custom-call | tf_op jit(solution)/shard_map/pallas_call | solution.py:568
  12.5 0.0 copy-done
  12.6 0.0 copy-done.2
  12.6 6.9 %shard_map.69 = (f32[2,384,768]{2,1,0:T(8,128)S(1)}, f32[2,128,128]{2,1,0:T(8,128)S(1)}) custom-call(s32[12]{0:T(128)S(1)} %get-tuple-element.23.rows, s32[12]{0:T(128)S(1)} %get-tuple-element.22.cols, s32[1]{0:T(128)} %bitcast.15.count, f32[2,384,768]{2,1,0:T(8,128)S(1)} %shard_map.68.extended.ext, f32[2,128,128]{2,1,0:T(8,128)S(1)} %copy-done.2, ...), custom_call_target="tpu_custom_call" | custom-call | tf_op jit(solution)/shard_map/pallas_call | solution.py:163
  19.5 17.3 %shard_map.70 = (f32[2,384,768]{2,1,0:T(8,128)S(1)}, f32[256,128]{1,0:T(8,128)S(1)}) custom-call(f32[2,384,768]{2,1,0:T(8,128)S(1)} %shard_map.68.extended.ext, f32[2,384,768]{2,1,0:T(8,128)S(1)} %get-tuple-element.10.grid, f32[256,128]{1,0:T(8,128)S(1)} %bitcast.19, f32[256,128]{1,0:T(8,128)S(1)} %bitcast.22), custom_call_target="tpu_custom_call" | custom-call | tf_op jit(solution)/shard_map/pallas_call | solution.py:568
  36.8 6.9 %shard_map.71 = (f32[2,384,768]{2,1,0:T(8,128)S(1)}, f32[2,128,128]{2,1,0:T(8,128)S(1)}) custom-call(s32[12]{0:T(128)S(1)} %get-tuple-element.23.rows, s32[12]{0:T(128)S(1)} %get-tuple-element.22.cols, s32[1]{0:T(128)} %bitcast.16.count, f32[2,384,768]{2,1,0:T(8,128)S(1)} %get-tuple-element.12.extended.ext, f32[2,128,128]{2,1,0:T(8,128)S(1)} %bitcast.20, ...), custom_call_target="tpu_custom_call" | custom-call | tf_op jit(solution)/shard_map/pallas_call | solution.py:163
  43.7 13.2 %shard_map.72 = (f32[2,256,512]{2,1,0:T(8,128)S(1)}, f32[256,128]{1,0:T(8,128)S(1)}) custom-call(f32[2,384,768]{2,1,0:T(8,128)S(1)} %get-tuple-element.12.extended.ext, f32[2,384,768]{2,1,0:T(8,128)S(1)} %get-tuple-element.14.grid, f32[256,128]{1,0:T(8,128)S(1)} %get-tuple-element.13.probe, f32[256,128]{1,0:T(8,128)S(1)} %bitcast.21), custom_call_target="tpu_custom_call" | custom-call | tf_op jit(solution)/shard_map/pallas_call | solution.py:568
  56.9 1.0 %copy.10 = f32[2,256,512]{2,1,0:T(8,128)} copy(f32[2,256,512]{2,1,0:T(8,128)S(1)} %get-tuple-element.28) | data formatting | bytes 2097152
  57.9 0.7 %copy.11 = f32[2,128,128]{2,1,0:T(8,128)} copy(f32[2,128,128]{2,1,0:T(8,128)S(1)} %bitcast.23) | data formatting | bytes 262144
  (1 shorter events, 0.0 us)
Async XLA Ops:
  0.6 2.2 %copy-start.1 = (f32[2,256,512]{2,1,0:T(8,128)S(1)}, f32[2,256,512]{2,1,0:T(8,128)}, u32[]{:S(2)}) copy-start(f32[2,256,512]{2,1,0:T(8,128)} %tile.1) | copy-start | bytes 3145732
  2.7 9.8 %copy-start = (f32[1,1,12,128,128]{4,3,2,1,0:T(8,128)S(1)}, f32[1,1,12,128,128]{4,3,2,1,0:T(8,128)}, u32[]{:S(2)}) copy-start(f32[1,1,12,128,128]{4,3,2,1,0:T(8,128)} %param.7) | copy-start | bytes 2359300
  2.7 9.8 %copy-start.2 = (f32[2,128,128]{2,1,0:T(8,128)S(1)}, f32[2,128,128]{2,1,0:T(8,128)}, u32[]{:S(2)}) copy-start(f32[2,128,128]{2,1,0:T(8,128)} %probe.1) | copy-start | bytes 393220

commit v2 on v1

--- a/solution.py
+++ b/solution.py
@@ -3,6 +3,7 @@
 
 import jax
 import jax.numpy as jnp
+import numpy as np
 from jax import lax
 from jax.experimental import pallas as pl
 from jax.experimental.pallas import tpu as pltpu
@@ -15,22 +16,23 @@
 step_probe = 0.5
 floor_amp = 0.5
 LANES = 128
+GROUP = 4
 
 
 def tables(size):
-    index = jnp.arange(size, dtype=jnp.int32)
-    wrapped = index[:, None] * index[None, :] % size
-    angle = 2.0 * math.pi / size * wrapped.astype(jnp.float32)
+    index = np.arange(size)
+    angle = 2.0 * math.pi / size * (index[:, None] * index[None, :] % size)
     scaling = 1.0 / math.sqrt(size)
-    cosine, sine = (jnp.cos(angle) * scaling, jnp.sin(angle) * scaling)
-    both = jnp.stack(
+    cosine, sine = (np.cos(angle) * scaling, np.sin(angle) * scaling)
+    both = np.stack(
         [
-            jnp.block([[cosine, -sine], [sine, cosine]]),
-            jnp.block([[cosine, sine], [-sine, cosine]]),
+            np.block([[cosine, -sine], [sine, cosine]]),
+            np.block([[cosine, sine], [-sine, cosine]]),
         ]
     )
-    high = lax.reduce_precision(both, 8, 7)
-    return (high.astype(jnp.bfloat16), (both - high).astype(jnp.bfloat16))
+    high = both.astype(jnp.bfloat16)
+    low = (both - high.astype(np.float64)).astype(jnp.bfloat16)
+    return (jnp.asarray(high), jnp.asarray(low))
 
 
 def split(value):
@@ -54,10 +56,13 @@
 
 def swap_blocks(value):
     n = LANES
+    down, across = value.shape[0] // n, value.shape[1] // n
     return jnp.concatenate(
         [
-            jnp.concatenate([value[:n, :n], value[n:, :n]], axis=1),
-            jnp.concatenate([value[:n, n:], value[n:, n:]], axis=1),
+            jnp.concatenate(
+                [value[i * n : (i + 1) * n, j * n : (j + 1) * n] for i in range(down)], axis=1
+            )
+            for j in range(across)
         ],
         axis=0,
     )
@@ -95,7 +100,7 @@
 
 
 def slots_kernel(
-    rows, cols, count, extended, probe, amplitude, high_tables, low_tables, grid, grad_probe
+    centres, count, extended, probe, amplitude, high_tables, low_tables, grid, grad_probe
 ):
     n = LANES
     slot_count = amplitude.shape[0]
@@ -106,13 +111,16 @@
     probe_sum_imag = jnp.zeros((n, n), jnp.float32)
     a_high, b_high = high_tables[0], high_tables[1]
     a_low, b_low = low_tables[0], low_tables[1]
-    for pair in range(slot_count // 2):
+    row_base = lax.axis_index("row") * (extended.shape[1] - n)
+    col_base = lax.axis_index("col") * (extended.shape[2] - 2 * n) - n // 2
+    for first in range(0, slot_count, GROUP):
+        group = range(first, first + GROUP)
         patches = []
         exits = []
         places = []
-        for slot in (2 * pair, 2 * pair + 1):
-            row_at = rows[slot]
-            col_at = cols[slot]
+        for slot in group:
+            row_at = centres[0, slot] - row_base
+            col_at = centres[1, slot] - col_base
             place = (
                 pl.multiple_of(row_at // 8 * 8, 8),
                 row_at % 8,
@@ -134,14 +142,14 @@
         wave = times_right(jnp.concatenate(exits, axis=0), a_high, a_low)
         far = times_left(b_high, b_low, swap_blocks(wave))
         far_real, far_imag = far[:n], far[n:]
-        measured = jnp.concatenate([amplitude[2 * pair], amplitude[2 * pair + 1]], axis=1)
+        measured = jnp.concatenate([amplitude[slot] for slot in group], axis=1)
         power = far_real * far_real + far_imag * far_imag
         keeping = 1.0 - measured * lax.rsqrt(jnp.maximum(power, floor_amp * floor_amp))
         kept = jnp.concatenate([far_real * keeping, far_imag * keeping], axis=0)
         back = times_left(a_high, a_low, kept)
         change = times_right(swap_blocks(back), b_high, b_low)
-        for k in range(2):
-            usable = jnp.where(2 * pair + k < count[0], 1.0, 0.0)
+        for k, slot in enumerate(group):
+            usable = jnp.where(slot < count[0, 0], 1.0, 0.0)
             change_real = change[k * n : (k + 1) * n, :n] * usable
             change_imag = change[k * n : (k + 1) * n, n:] * usable
             object_real, object_imag = patches[k]
@@ -157,7 +165,7 @@
     grad_probe[1] = probe_sum_imag
 
 
-def gradients(rows, cols, count, extended, probe, amplitude, high_tables, low_tables):
+def gradients(centres, count, extended, probe, amplitude, high_tables, low_tables):
     smem = pl.BlockSpec(memory_space=pltpu.SMEM)
     vmem = pl.BlockSpec(memory_space=pltpu.VMEM)
     return pl.pallas_call(
@@ -166,10 +174,10 @@
             jax.ShapeDtypeStruct(extended.shape, jnp.float32),
             jax.ShapeDtypeStruct(probe.shape, jnp.float32),
         ),
-        in_specs=[smem] * 3 + [vmem] * 5,
+        in_specs=[smem] * 2 + [vmem] * 5,
         out_specs=(vmem, vmem),
         compiler_params=pltpu.CompilerParams(vmem_limit_bytes=40 * 1024 * 1024),
-    )(rows, cols, count, extended, probe, amplitude, high_tables, low_tables)
+    )(centres, count, extended, probe, amplitude, high_tables, low_tables)
 
 
 MESH = pl.DeviceIdType.MESH
@@ -590,8 +598,6 @@
     recorded = sizes["row"] * sizes["col"] * (2 * slot_count // 3)
     scaling = step_probe / recorded
     high_tables, low_tables = tables(n)
-    start_rows = positions[0, 0, 0] - lax.axis_index("row") * tile_rows
-    start_cols = positions[0, 0, 1] - lax.axis_index("col") * tile_cols + half
     measured = amplitudes[0, 0]
     wide = (2, tile_rows + n, tile_cols + 2 * n)
     share = 2 * n // sizes["row"]
@@ -605,7 +611,7 @@
     )
     for iteration in range(ITERS):
         grid, grad_probe = gradients(
-            start_rows, start_cols, counts[0], extended, probe_field, measured,
+            positions[0, 0], counts, extended, probe_field, measured,
             high_tables, low_tables,
         )
         operands = (

time: 58.7 us -> 55.3 us (0.942)
  Pallas kernels: 54 us -> 50.8 us
  other arithmetic: 1.42 us -> 0 us
  local copies, waits for them, and re-layouts: 1.64 us -> 2.87 us
    pallas_call x2, Pallas kernels: 13.8 us -> 10.7 us  [gradients(): pl.pallas_call(slots_kernel, out_shape=(jax.ShapeDtypeStruct(extended.sha...]
    unnamed x8 -> x14, local copies, waits for them, and re-layouts: 1.64 us -> 2.87 us
    add x1 -> x0, other arithmetic: 0.76 us -> none  [shards(): start_cols = positions[0, 0, 1] - lax.axis_index('col') * tile_cols + half]
where the time goes in v2:
time: 55.3 us; the launch traced here: 55.1 us
  Pallas kernels  50.8 us (92%)
  local copies, waits for them, and re-layouts  2.87 us (5%)
  between operations  1.49 us (3%)
    pallas_call x3, Pallas kernels, remote(): pl.pallas_call(kernel, out_shape=[jax.ShapeDtypeStruct(shape, jnp.float32...  40.1 us
    pallas_call x2, Pallas kernels, gradients(): pl.pallas_call(slots_kernel, out_shape=(jax.ShapeDtypeStruct(extended.sha...  10.7 us
    unnamed x14, local copies, waits for them, and re-layouts  2.87 us

profile of v2, /device:TPU:0, one launch (start us, length us, event | category | flops | bytes accessed | tf_op | source)
XLA Modules:
  0.0 55.1 jit_solution(5357648661391523058)
XLA Ops:
  0.6 0.0 copy-start.1
  0.6 0.0 copy-start.2
  0.7 0.0 copy-start
  1.4 0.0 copy-start.3
  1.4 1.2 %copy-done.3 = f32[2,256,512]{2,1,0:T(8,128)S(1)} copy-done((f32[2,256,512]{2,1,0:T(8,128)S(1)}, f32[2,256,512]{2,1,0:T(8,128)}, u32[]{:S(2)}) %copy-start.3) | copy-done | bytes 1048600
  2.6 0.0 copy-start.4
  2.6 0.0 copy-start.5
  2.6 9.6 %shard_map.86.extended.ext = f32[2,384,768]{2,1,0:T(8,128)S(1)} custom-call(f32[2,256,512]{2,1,0:T(8,128)S(1)} %copy-done.3), custom_call_target="tpu_custom_call" | custom-call | tf_op jit(solution)/shard_map/pallas_call | solution.py:576
  12.3 0.0 copy-done.1
  12.3 0.0 copy-done.2
  12.3 0.0 copy-done
  12.3 0.0 copy-done.4
  12.3 0.0 copy-done.5
  12.3 5.3 %shard_map.87 = (f32[2,384,768]{2,1,0:T(8,128)S(1)}, f32[2,128,128]{2,1,0:T(8,128)S(1)}) custom-call(s32[2,12]{1,0:T(2,128)S(1)} %bitcast.14, s32[1,1]{1,0:T(1,128)S(6)} %copy.11.count, f32[2,384,768]{2,1,0:T(8,128)S(1)} %shard_map.86.extended.ext, f32[2,128,128]{2,1,0:T(8,128)S(1)} %copy-done.4, f32[12,128,128]{2,1,0:T(8,128)S(1)} %bitcast.7, ...), custom_call_target="tpu_custom_call" | custom-call | tf_op jit(solution)/shard_map/pallas_call | solution.py:171
  17.7 17.3 %shard_map.88 = (f32[2,384,768]{2,1,0:T(8,128)S(1)}, f32[256,128]{1,0:T(8,128)S(1)}) custom-call(f32[2,384,768]{2,1,0:T(8,128)S(1)} %shard_map.86.extended.ext, f32[2,384,768]{2,1,0:T(8,128)S(1)} %get-tuple-element.10.grid, f32[256,128]{1,0:T(8,128)S(1)} %bitcast.9, f32[256,128]{1,0:T(8,128)S(1)} %bitcast.12), custom_call_target="tpu_custom_call" | custom-call | tf_op jit(solution)/shard_map/pallas_call | solution.py:576
  34.9 5.3 %shard_map.89 = (f32[2,384,768]{2,1,0:T(8,128)S(1)}, f32[2,128,128]{2,1,0:T(8,128)S(1)}) custom-call(s32[2,12]{1,0:T(2,128)S(1)} %bitcast.15, s32[1,1]{1,0:T(1,128)S(6)} %copy.11.count, f32[2,384,768]{2,1,0:T(8,128)S(1)} %get-tuple-element.12.extended.ext, f32[2,128,128]{2,1,0:T(8,128)S(1)} %bitcast.10, f32[12,128,128]{2,1,0:T(8,128)S(1)} %bitcast.8, ...), custom_call_target="tpu_custom_call" | custom-call | tf_op jit(solution)/shard_map/pallas_call | solution.py:171
  40.3 13.2 %shard_map.90 = (f32[2,256,512]{2,1,0:T(8,128)S(1)}, f32[256,128]{1,0:T(8,128)S(1)}) custom-call(f32[2,384,768]{2,1,0:T(8,128)S(1)} %get-tuple-element.12.extended.ext, f32[2,384,768]{2,1,0:T(8,128)S(1)} %get-tuple-element.14.grid, f32[256,128]{1,0:T(8,128)S(1)} %get-tuple-element.13.probe, f32[256,128]{1,0:T(8,128)S(1)} %bitcast.11), custom_call_target="tpu_custom_call" | custom-call | tf_op jit(solution)/shard_map/pallas_call | solution.py:576
  53.5 1.0 %copy.12 = f32[2,256,512]{2,1,0:T(8,128)} copy(f32[2,256,512]{2,1,0:T(8,128)S(1)} %get-tuple-element.20) | data formatting | bytes 2097152
  54.5 0.7 %copy.13 = f32[2,128,128]{2,1,0:T(8,128)} copy(f32[2,128,128]{2,1,0:T(8,128)S(1)} %bitcast.13) | data formatting | bytes 262144
Async XLA Ops:
  0.6 11.7 %copy-start.1 = (bf16[2,256,256]{2,1,0:T(8,128)(2,1)S(1)}, bf16[2,256,256]{2,1,0:T(8,128)(2,1)}, u32[]{:S(2)}) copy-start(bf16[2,256,256]{2,1,0:T(8,128)(2,1)} %constant.5.clone.low_tables) | copy-start | bytes 786436
  0.6 11.7 %copy-start.2 = (bf16[2,256,256]{2,1,0:T(8,128)(2,1)S(1)}, bf16[2,256,256]{2,1,0:T(8,128)(2,1)}, u32[]{:S(2)}) copy-start(bf16[2,256,256]{2,1,0:T(8,128)(2,1)} %constant.4.clone.high_tables) | copy-start | bytes 786436
  0.7 11.7 %copy-start = (f32[1,1,12,128,128]{4,3,2,1,0:T(8,128)S(1)}, f32[1,1,12,128,128]{4,3,2,1,0:T(8,128)}, u32[]{:S(2)}) copy-start(f32[1,1,12,128,128]{4,3,2,1,0:T(8,128)} %param.9) | copy-start | bytes 2359300
  1.4 1.2 %copy-start.3 = (f32[2,256,512]{2,1,0:T(8,128)S(1)}, f32[2,256,512]{2,1,0:T(8,128)}, u32[]{:S(2)}) copy-start(f32[2,256,512]{2,1,0:T(8,128)} %tile.1) | copy-start | bytes 3145732
  2.6 9.7 %copy-start.4 = (f32[2,128,128]{2,1,0:T(8,128)S(1)}, f32[2,128,128]{2,1,0:T(8,128)}, u32[]{:S(2)}) copy-start(f32[2,128,128]{2,1,0:T(8,128)} %probe.1) | copy-start | bytes 393220
  2.6 9.7 %copy-start.5 = (s32[1,1,2,12]{3,2,1,0:T(2,128)S(1)}, s32[1,1,2,12]{3,2,1,0:T(2,128)}, u32[]{:S(2)}) copy-start(s32[1,1,2,12]{3,2,1,0:T(2,128)} %param.10) | copy-start | bytes 292

commit v3 on v2

--- a/solution.py
+++ b/solution.py
@@ -260,16 +260,21 @@
 STEPS = (-1, 1)
 
 
-def halo_kernel(sizes, tile, ext, band_out, band_in, corner_out, corner_in, send_sem, recv_sem):
+def halo_kernel(sizes, tile, ext, band_out, band_in, corner_out, corner_in, send_sem, recv_sem, local_sem):
     n = LANES
     half = n // 2
     tile_rows, tile_cols = tile.shape[1:]
     last = tile_cols + n
+    inside = pltpu.make_async_copy(
+        tile, ext.at[:, pl.ds(half, tile_rows), pl.ds(n, tile_cols)], local_sem
+    )
+    inside.start()
     links = Links(sizes, send_sem, recv_sem)
     links.greet(False)
+    inside.wait()
     rows = []
     for step in STEPS:
-        src = tile.at[:, pl.ds(0 if step < 0 else tile_rows - half, half), :]
+        src = ext.at[:, pl.ds(half if step < 0 else tile_rows, half), pl.ds(n, tile_cols)]
         to = tile_rows + half if step < 0 else 0
         rows.append(
             links.edge(src, ext.at[:, pl.ds(to, half), pl.ds(n, tile_cols)], "row", step)
@@ -277,9 +282,9 @@
     lane = lax.broadcasted_iota(jnp.int32, (tile_rows, n), 1)
     bands = []
     for k, step in enumerate(STEPS):
-        at = 0 if step < 0 else tile_cols - n
-        real = tile[0, :, at : at + n]
-        imag = pltpu.roll(tile[1, :, at : at + n], half, 1)
+        at = n if step < 0 else tile_cols
+        real = ext[0, half : half + tile_rows, at : at + n]
+        imag = pltpu.roll(ext[1, half : half + tile_rows, at : at + n], half, 1)
         low, high = (real, imag) if step < 0 else (imag, real)
         band_out[k] = jnp.where(lane < half, low, high)
         clear(links, "col", -step, band_in.at[k])
@@ -292,7 +297,6 @@
         clear(links, "row", -step, corner_in.at[k])
         to = tile_rows + half if step < 0 else 0
         clear(links, "row", -step, ext.at[:, pl.ds(to, half), pl.ds(n, tile_cols)])
-    ext[:, half : half + tile_rows, n : n + tile_cols] = tile[...]
     for k, step in enumerate(STEPS):
         bands[k].wait_recv()
         got = band_in[k]
@@ -571,15 +575,16 @@
     summed.finish()
 
 
-def remote(kernel, collective_id, sizes, outs, scratch, copies, *operands):
+def remote(kernel, collective_id, sizes, outs, scratch, copies, *operands, place=pltpu.VMEM, more=()):
     vmem = pl.BlockSpec(memory_space=pltpu.VMEM)
     return pl.pallas_call(
         kernel,
         out_shape=[jax.ShapeDtypeStruct(shape, jnp.float32) for shape in outs],
-        in_specs=[vmem] * len(operands),
+        in_specs=[pl.BlockSpec(memory_space=place)] * len(operands),
         out_specs=[vmem] * len(outs),
         scratch_shapes=[pltpu.VMEM(shape, jnp.float32) for shape in scratch]
-        + [pltpu.SemaphoreType.DMA((copies,))] * 2,
+        + [pltpu.SemaphoreType.DMA((copies,))] * 2
+        + list(more),
         compiler_params=pltpu.CompilerParams(
             collective_id=collective_id,
             has_side_effects=True,
@@ -608,6 +613,7 @@
     (extended,) = remote(
         functools.partial(halo_kernel, sizes), 0, sizes, [wide],
         [(2, tile_rows, n)] * 2 + [(2, 2, half, n)] * 2, 6, object_field,
+        place=pltpu.HBM, more=(pltpu.SemaphoreType.DMA,),
     )
     for iteration in range(ITERS):
         grid, grad_probe = gradients(

time: 55.3 us -> 55.5 us (level)
  no operation moved by 1% of the time
where the time goes in v3:
time: 55.5 us; the launch traced here: 55.3 us
  Pallas kernels  50.9 us (92%)
  local copies, waits for them, and re-layouts  2.87 us (5%)
  between operations  1.49 us (3%)
    pallas_call x3, Pallas kernels, remote(): pl.pallas_call(kernel, out_shape=[jax.ShapeDtypeStruct(shape, jnp.float32...  40.3 us
    pallas_call x2, Pallas kernels, gradients(): pl.pallas_call(slots_kernel, out_shape=(jax.ShapeDtypeStruct(extended.sha...  10.6 us
    unnamed x14, local copies, waits for them, and re-layouts  2.87 us

profile of v3, /device:TPU:0, one launch (start us, length us, event | category | flops | bytes accessed | tf_op | source)
XLA Modules:
  0.0 55.3 jit_solution(7092782424107931801)
XLA Ops:
  0.6 0.0 copy-start.1
  0.6 0.0 copy-start.2
  0.7 0.0 copy-start
  1.4 0.0 copy-start.3
  1.4 1.2 %copy-done.3 = f32[2,256,512]{2,1,0:T(8,128)S(1)} copy-done((f32[2,256,512]{2,1,0:T(8,128)S(1)}, f32[2,256,512]{2,1,0:T(8,128)}, u32[]{:S(2)}) %copy-start.3) | copy-done | bytes 1048600
  2.6 0.0 copy-start.4
  2.6 0.0 copy-start.5
  2.6 9.8 %shard_map.86.extended.ext = f32[2,384,768]{2,1,0:T(8,128)S(1)} custom-call(f32[2,256,512]{2,1,0:T(8,128)S(1)} %copy-done.3), custom_call_target="tpu_custom_call" | custom-call | tf_op jit(solution)/shard_map/pallas_call | solution.py:580
  12.5 0.0 copy-done.1
  12.5 0.0 copy-done.2
  12.5 0.0 copy-done
  12.5 0.0 copy-done.4
  12.5 0.0 copy-done.5
  12.5 5.3 %shard_map.87 = (f32[2,384,768]{2,1,0:T(8,128)S(1)}, f32[2,128,128]{2,1,0:T(8,128)S(1)}) custom-call(s32[2,12]{1,0:T(2,128)S(1)} %bitcast.14, s32[1,1]{1,0:T(1,128)S(6)} %copy.11.count, f32[2,384,768]{2,1,0:T(8,128)S(1)} %shard_map.86.extended.ext, f32[2,128,128]{2,1,0:T(8,128)S(1)} %copy-done.4, f32[12,128,128]{2,1,0:T(8,128)S(1)} %bitcast.7, ...), custom_call_target="tpu_custom_call" | custom-call | tf_op jit(solution)/shard_map/pallas_call | solution.py:171
  17.8 17.3 %shard_map.88 = (f32[2,384,768]{2,1,0:T(8,128)S(1)}, f32[256,128]{1,0:T(8,128)S(1)}) custom-call(f32[2,384,768]{2,1,0:T(8,128)S(1)} %shard_map.86.extended.ext, f32[2,384,768]{2,1,0:T(8,128)S(1)} %get-tuple-element.10.grid, f32[256,128]{1,0:T(8,128)S(1)} %bitcast.9, f32[256,128]{1,0:T(8,128)S(1)} %bitcast.12), custom_call_target="tpu_custom_call" | custom-call | tf_op jit(solution)/shard_map/pallas_call | solution.py:580
  35.1 5.3 %shard_map.89 = (f32[2,384,768]{2,1,0:T(8,128)S(1)}, f32[2,128,128]{2,1,0:T(8,128)S(1)}) custom-call(s32[2,12]{1,0:T(2,128)S(1)} %bitcast.15, s32[1,1]{1,0:T(1,128)S(6)} %copy.11.count, f32[2,384,768]{2,1,0:T(8,128)S(1)} %get-tuple-element.12.extended.ext, f32[2,128,128]{2,1,0:T(8,128)S(1)} %bitcast.10, f32[12,128,128]{2,1,0:T(8,128)S(1)} %bitcast.8, ...), custom_call_target="tpu_custom_call" | custom-call | tf_op jit(solution)/shard_map/pallas_call | solution.py:171
  40.5 13.2 %shard_map.90 = (f32[2,256,512]{2,1,0:T(8,128)S(1)}, f32[256,128]{1,0:T(8,128)S(1)}) custom-call(f32[2,384,768]{2,1,0:T(8,128)S(1)} %get-tuple-element.12.extended.ext, f32[2,384,768]{2,1,0:T(8,128)S(1)} %get-tuple-element.14.grid, f32[256,128]{1,0:T(8,128)S(1)} %get-tuple-element.13.probe, f32[256,128]{1,0:T(8,128)S(1)} %bitcast.11), custom_call_target="tpu_custom_call" | custom-call | tf_op jit(solution)/shard_map/pallas_call | solution.py:580
  53.7 1.0 %copy.12 = f32[2,256,512]{2,1,0:T(8,128)} copy(f32[2,256,512]{2,1,0:T(8,128)S(1)} %get-tuple-element.20) | data formatting | bytes 2097152
  54.7 0.7 %copy.13 = f32[2,128,128]{2,1,0:T(8,128)} copy(f32[2,128,128]{2,1,0:T(8,128)S(1)} %bitcast.13) | data formatting | bytes 262144
Async XLA Ops:
  0.6 11.8 %copy-start.1 = (bf16[2,256,256]{2,1,0:T(8,128)(2,1)S(1)}, bf16[2,256,256]{2,1,0:T(8,128)(2,1)}, u32[]{:S(2)}) copy-start(bf16[2,256,256]{2,1,0:T(8,128)(2,1)} %constant.5.clone.low_tables) | copy-start | bytes 786436
  0.6 11.8 %copy-start.2 = (bf16[2,256,256]{2,1,0:T(8,128)(2,1)S(1)}, bf16[2,256,256]{2,1,0:T(8,128)(2,1)}, u32[]{:S(2)}) copy-start(bf16[2,256,256]{2,1,0:T(8,128)(2,1)} %constant.4.clone.high_tables) | copy-start | bytes 786436
  0.7 11.8 %copy-start = (f32[1,1,12,128,128]{4,3,2,1,0:T(8,128)S(1)}, f32[1,1,12,128,128]{4,3,2,1,0:T(8,128)}, u32[]{:S(2)}) copy-start(f32[1,1,12,128,128]{4,3,2,1,0:T(8,128)} %param.9) | copy-start | bytes 2359300
  1.4 1.2 %copy-start.3 = (f32[2,256,512]{2,1,0:T(8,128)S(1)}, f32[2,256,512]{2,1,0:T(8,128)}, u32[]{:S(2)}) copy-start(f32[2,256,512]{2,1,0:T(8,128)} %tile.1) | copy-start | bytes 3145732
  2.6 9.9 %copy-start.4 = (f32[2,128,128]{2,1,0:T(8,128)S(1)}, f32[2,128,128]{2,1,0:T(8,128)}, u32[]{:S(2)}) copy-start(f32[2,128,128]{2,1,0:T(8,128)} %probe.1) | copy-start | bytes 393220
  2.6 9.9 %copy-start.5 = (s32[1,1,2,12]{3,2,1,0:T(2,128)S(1)}, s32[1,1,2,12]{3,2,1,0:T(2,128)}, u32[]{:S(2)}) copy-start(s32[1,1,2,12]{3,2,1,0:T(2,128)} %param.10) | copy-start | bytes 292
